TPU v7x, 512 devices: a whole 4x4x16 slice. The times are simulated.
512 devices in a mesh: req: 128 (over z, y_lo, x), tp: 4 (over y_hi, core).
Axes of the slice: x: 4, y: 4 (y_hi: 2, y_lo: 2; y = y_hi * 2 + y_lo), z: 16, core: 2. Of those that a mesh axis runs over, the one named last changes fastest.
Arguments:
- hidden: bfloat16 [8192, 2048], P('req'), may hold values from -6 to 6
- draft_query: bfloat16 [8192, 2048], P('req', 'tp'), may hold values from -180 to 180
- draft_kv: bfloat16 [2, 8192, 2048], P(None, 'req', 'tp'), may hold values from -6 to 6
- cache_kv: bfloat16 [2, 32768, 2048], P(None, 'req', 'tp'), may hold values from -6 to 6
- piece_offset: int32 [256], P('req'), may hold values from 0 to 3
- piece_length: int32 [256], P('req'), may hold values from 1 to 128
- ancestors: int32 [8192, 64], P('req'), may hold values from 0 to 1, as said below
- out_proj: bfloat16 [2048, 2048], P('tp'), may hold values from -0.125 to 0.125
- ffn_gain: float32 [2048], replicated, may hold values from 0.1 to 1.9
- router_w: bfloat16 [2048, 64], replicated, may hold values from -0.125 to 0.125
- expert_gate_up: bfloat16 [2, 2048, 65536], P(None, None, ('req', 'tp')), may hold values from -0.125 to 0.125
- expert_down: bfloat16 [65536, 2048], P(('req', 'tp')), may hold values from -1.5 to 1.5
- expert_ids: int32 [8192, 8], P('req'), may hold values from 0 to 63, all different within a row; in each aligned block of 64 rows (0 to 63, 64 to 127, ...) at most 12 rows name the same one
- accepted_ids: int32 [1024], P('req'), may hold values from 0 to 63
Outputs:
- layer_out: bfloat16 [8192, 2048], P('req', 'tp')
- attended: bfloat16 [8192, 2048], P('req', 'tp')
- accepted_kv: bfloat16 [2, 1024, 2048], P(None, 'req', 'tp')
Inputs may be any that keep to these rules, and one draw needn't show every extreme that they name: Piece p of device d belongs to the request of device (d - piece_offset[p]) mod 128. Within each request's 64 rows, row i marks node i and all its ancestors; node 0 is the root and every other node's parent has a lower number. `expert_ids`: each row names 8 different experts; in the rows of one device no expert is named by more than 12 rows, a bound that some block reaches.
All inputs are finite; a program needn't handle non-finite values.
Results may differ from a plain program's by a relative error of at most 0.03.
Values may be sent and summed in bfloat16 or wider, within the bound.
A program may use at most 64 MiB of HBM per device.

v0:
```python
import jax
import jax.numpy as jnp
from jax import lax
from jax.sharding import PartitionSpec as P

HD = 128
PIECES = 2
PIECE = 128
SPAN = 4


NEG = -1e30


def passed_along(value, axis, by):
    devices = lax.axis_size(axis)
    return lax.ppermute(value, axis, [(i, (i + by) % devices) for i in range(devices)])


def partials(scores, mask, values, equation):
    top = jnp.max(jnp.where(mask, scores, NEG), axis=-1)
    weights = jnp.where(mask, jnp.exp(scores - top[..., None]), 0.0)
    total = jnp.sum(weights, axis=-1)
    acc = jnp.einsum(
        equation, weights.astype(jnp.bfloat16), values, preferred_element_type=jnp.float32
    )
    return (top, total, acc)


def finish_expert(gate, upper, expert_down, shape):
    act = (jax.nn.silu(gate) * upper).astype(jnp.bfloat16)
    result = (
        jnp.dot(act, expert_down, preferred_element_type=jnp.float32)
        .astype(jnp.bfloat16)
        .reshape(shape)
    )
    return lax.all_to_all(result, "req", split_axis=0, concat_axis=0, tiled=True)


def body(
    hidden,
    draft_query,
    draft_kv,
    cache_kv,
    piece_offset,
    piece_length,
    ancestors,
    out_proj,
    ffn_gain,
    router_w,
    expert_gate_up,
    expert_down,
    expert_ids,
    accepted_ids,
):
    rows = hidden.shape[0]
    local_heads = draft_query.shape[1] // HD
    scale = HD ** (-0.5)
    query = draft_query.reshape(rows, local_heads, HD)
    own_keys = draft_kv[0].reshape(rows, local_heads, HD)
    own_values = draft_kv[1].reshape(rows, local_heads, HD)
    pieces = cache_kv.reshape(2, PIECES, PIECE, local_heads, HD)
    slots = jnp.arange(PIECE, dtype=jnp.int32)
    dscores = (
        jnp.einsum("thd,shd->ths", query, own_keys, preferred_element_type=jnp.float32) * scale
    )
    dtop, dtotal, dacc = partials(dscores, (ancestors > 0)[:, None, :], own_values, "ths,shd->thd")
    parts = [(dtop[None], dtotal[None], dacc[None])]
    tags = jnp.stack([piece_offset, piece_length]).astype(jnp.bfloat16)
    for step in range(SPAN):
        if step == 0:
            kv_here, tag_here = (pieces, tags)
        else:
            kv_here, tag_here = passed_along((pieces, tags), "req", -step)
        valid = (tag_here[0] == step)[:, None] & (
            slots[None, :].astype(jnp.float32) < tag_here[1].astype(jnp.float32)[:, None]
        )
        scores = (
            jnp.einsum("thd,pshd->pths", query, kv_here[0], preferred_element_type=jnp.float32)
            * scale
        )
        parts.append(partials(scores, valid[:, None, None, :], kv_here[1], "pths,pshd->pthd"))
    tops = jnp.concatenate([item[0] for item in parts])
    totals = jnp.concatenate([item[1] for item in parts])
    accs = jnp.concatenate([item[2] for item in parts])
    best = jnp.max(tops, axis=0)
    factor = jnp.exp(tops - best[None])
    merged = jnp.sum(factor[..., None] * accs, axis=0) / jnp.sum(factor * totals, axis=0)[..., None]
    attended = merged.astype(jnp.bfloat16).reshape(rows, local_heads * HD)
    partial_proj = jnp.dot(attended, out_proj, preferred_element_type=jnp.float32)
    attn_proj = lax.psum(partial_proj.astype(jnp.bfloat16), "tp").astype(jnp.float32)
    residual = (hidden.astype(jnp.float32) + attn_proj).astype(jnp.bfloat16)
    resf = residual.astype(jnp.float32)
    normed = (
        resf * lax.rsqrt(jnp.mean(resf * resf, axis=1, keepdims=True) + 1e-06) * ffn_gain
    ).astype(jnp.bfloat16)
    logits = jnp.dot(normed, router_w, preferred_element_type=jnp.float32)
    experts = router_w.shape[1]
    top_count = expert_ids.shape[1]
    picks = expert_ids[:, :, None] == jnp.arange(experts, dtype=jnp.int32)
    chosen = jnp.sum(jnp.where(picks, logits[:, None, :], 0.0), axis=2)
    gates = jax.nn.softmax(chosen, axis=1).astype(jnp.bfloat16)
    routed = jnp.sum(picks.astype(jnp.int32), axis=1)
    gate_of = jnp.sum(jnp.where(picks, gates.astype(jnp.float32)[:, :, None], 0.0), axis=1)
    capacity = min(rows, 3 * ((rows * top_count + experts - 1) // experts) // 2)
    rank = jnp.cumsum(routed, axis=0) - routed
    placed = (routed[:, :, None] > 0) & (rank[:, :, None] == jnp.arange(capacity, dtype=jnp.int32))
    outgoing = jnp.einsum(
        "tec,tm->ecm", placed.astype(jnp.bfloat16), normed, preferred_element_type=jnp.float32
    ).astype(jnp.bfloat16)
    outgoing = jnp.repeat(outgoing, 2, axis=0)
    received = lax.all_to_all(outgoing, "req", split_axis=0, concat_axis=0, tiled=True)
    flat = received.reshape(-1, received.shape[2])
    gate = jnp.dot(flat, expert_gate_up[0], preferred_element_type=jnp.float32)
    upper = jnp.dot(flat, expert_gate_up[1], preferred_element_type=jnp.float32)
    returned = finish_expert(gate, upper, expert_down, received.shape)
    weighting = jnp.repeat(
        (placed.astype(jnp.float32) * gate_of[:, :, None]).astype(jnp.bfloat16), 2, axis=1
    )
    moe_part = jnp.einsum("tdc,dcm->tm", weighting, returned, preferred_element_type=jnp.float32)
    moe = lax.psum_scatter(
        moe_part.astype(jnp.bfloat16), "tp", scatter_dimension=1, tiled=True
    ).astype(jnp.float32)
    cols = moe.shape[1]
    residual_part = lax.dynamic_slice_in_dim(resf, lax.axis_index("tp") * cols, cols, 1)
    layer_out = (residual_part + moe).astype(jnp.bfloat16)
    accepted_kv = jnp.take(draft_kv, accepted_ids, axis=1)
    return (layer_out, attended, accepted_kv)


def solution(mesh):
    in_specs = (
        P("req", None),
        P("req", "tp"),
        P(None, "req", "tp"),
        P(None, "req", "tp"),
        P("req"),
        P("req"),
        P("req", None),
        P("tp", None),
        P(),
        P(),
        P(None, None, ("req", "tp")),
        P(("req", "tp"), None),
        P("req", None),
        P("req"),
    )
    out_specs = (P("req", "tp"), P("req", "tp"), P(None, "req", "tp"))
    return jax.shard_map(body, mesh=mesh, in_specs=in_specs, out_specs=out_specs, check_vma=False)
```

profile of v0, /device:TPU:6, one launch (start us, length us, event | category | flops | bytes accessed | tf_op | source)
XLA Modules:
  0.0 1011.0 jit_solution(13778763631182478897)
XLA Ops:
  7.3 0.8 convert_bitcast_fusion
  8.1 0.7 convert_bitcast_fusion.1
  8.7 0.5 pad_maximum_fusion
  9.3 7.7 collective-permute-start.4
  17.0 8.9 collective-permute-start.2
  25.9 1.9 collective-permute-start
  27.8 1.2 reshape.364
  29.0 0.9 copy.162
  29.9 3.0 collective-permute-start.1
  32.9 4.0 collective-permute-start.5
  36.9 0.7 compare_bitcast_fusion.3
  37.5 0.5 iota_convert_fusion
  38.1 1.8 fusion.77
  39.8 0.6 reshape.363
  40.5 0.8 squeeze.38
  41.6 0.6 fusion.55
  42.5 1.0 squeeze.42
  43.5 0.7 copy.180
  44.2 5.4 collective-permute-start.3
  49.6 0.6 bitcast_convert_fusion
  50.2 0.6 compare_bitcast_fusion
  50.9 0.6 bitcast_convert_fusion.1
  51.5 0.6 compare_bitcast_fusion.1
  52.1 0.6 bitcast_convert_fusion.2
  52.7 0.6 compare_bitcast_fusion.2
  53.4 0.7 compare_and_fusion.1
  54.1 1.9 select_reduce_fusion.9
  56.0 10.6 %collective-permute-done.5 = bf16[2,2,128,4,128]{4,2,1,3,0:T(8,128)(2,1)} collective-permute-done((bf16[2,2,128,4,128]{4,2,1,3,0:T(8,128)(2,1)}, bf16[2,2,128,4,128]{4,2,1,3,0:T(8,128)(2,1)}, u32[]{:S(2)}, u32[]{:S(2)}) %collective-permute-start.5) | collective-permute-done | bytes 524320 | tf_op jit(solution)/shard_map/ppermute | solution.py:17
  66.6 1.3 select_reduce_fusion.3
  67.9 1.4 fusion.47
  69.3 1.2 select_reduce_fusion.5
  70.5 1.4 fusion.45
  72.0 2.5 select_reduce_fusion.7
  74.4 2.7 concatenate.16
  77.1 2.6 fusion.41
  79.7 0.7 maximum_maximum_fusion
  80.4 2.7 concatenate.18
  83.1 0.8 multiply_reduce_fusion.2
  84.0 1.1 fusion.12
  85.1 1.3 fusion.11
  86.3 1.2 fusion.10
  87.6 1.2 fusion.9
  88.8 0.4 multiply_reduce_fusion
  89.3 1.2 convolution_convert_fusion.2
  90.5 0.9 convert_reduce_fusion
  91.7 54.2 %all-reduce.2.cloned.1.call-done = bf16[64,2048]{1,0:T(8,128)(2,1)} async-done(((bf16[64,2048]{1,0:T(8,128)(2,1)}), bf16[64,2048]{1,0:T(8,128)(2,1)}) %all-reduce.2.cloned.1.call-update) | async-done | bytes 262160 | tf_op jit(solution)/shard_map/psum | solution.py:91
  146.0 1.9 fusion.34
  147.9 2.0 convolution_convert_fusion.1
  149.9 1.8 copy.187
  151.7 4.3 broadcast_in_dim.165
  156.0 381.7 %all_to_all.10 = bf16[128,12,2048]{2,1,0:T(8,128)(2,1)} all-to-all(bf16[128,12,2048]{2,1,0:T(8,128)(2,1)} %bitcast.127), channel_id=1, replica_groups=mesh['req'=128,'tp'=4] {'req'}, dimensions={0} | all-to-all | bytes 12582912 | tf_op jit(solution)/shard_map/all_to_all | solution.py:112
  537.7 10.8 %reshape.367 = bf16[1536,2048]{1,0:T(8,128)(2,1)} reshape(bf16[128,12,2048]{2,1,0:T(8,128)(2,1)} %all_to_all.10) | data formatting | bytes 12582912 | tf_op jit(solution)/shard_map/reshape | solution.py:113
  548.5 4.6 fusion.26
  553.2 11.9 %convolution_convert_fusion = bf16[1536,2048]{1,0:T(8,128)(2,1)} fusion(bf16[128,2048]{1,0:T(8,128)(2,1)S(1)} %copy-done.4, bf16[1536,2048]{1,0:T(8,128)(2,1)} %reshape.367, f32[1536,128]{1,0:T(8,128)S(1)} %fusion.26, bf16[2,2048,128]{2,1,0:T(8,128)(2,1)S(1)} %copy-done.8), kind=kOutput, calls=%fused_computation.1 | convolution fusion | flops 1614938112 | bytes 14417920 | tf_op jit(solution)/shard_map/dot_general | solution.py:33
  565.0 10.6 %reshape.368 = bf16[128,12,2048]{2,1,0:T(8,128)(2,1)} reshape(bf16[1536,2048]{1,0:T(8,128)(2,1)} %convolution_convert_fusion) | data formatting | bytes 12582912 | tf_op jit(solution)/shard_map/reshape | solution.py:35
  575.6 12.8 %all-to-all-start.1 = ((bf16[128,12,2048]{2,1,0:T(8,128)(2,1)}), bf16[128,12,2048]{2,1,0:T(8,128)(2,1)}, u32[]{:S(2)}, u32[]{:S(2)}) async-start(bf16[128,12,2048]{2,1,0:T(8,128)(2,1)} %reshape.368), calls=%async_computation.1 | async-start | bytes 16777216 | tf_op jit(solution)/shard_map/all_to_all | solution.py:37
  588.7 0.3 fusion.74
  590.0 363.6 %all-to-all-done.1 = bf16[128,12,2048]{2,1,0:T(8,128)(2,1)} async-done(((bf16[128,12,2048]{2,1,0:T(8,128)(2,1)}), bf16[128,12,2048]{2,1,0:T(8,128)(2,1)}, u32[]{:S(2)}, u32[]{:S(2)}) %all-to-all-start.1) | async-done | bytes 6291488 | tf_op jit(solution)/shard_map/all_to_all | solution.py:37
  953.6 0.3 broadcast_in_dim.164
  953.9 11.2 %fusion.6 = bf16[64,2048]{1,0:T(8,128)(2,1)} fusion(bf16[64,128,12]{0,1,2:T(8,128)(2,1)S(1)} %bitcast.128, bf16[128,12,2048]{2,1,0:T(8,128)(2,1)} %all-to-all-done.1), kind=kOutput, calls=%fused_computation.8 | convolution fusion | flops 402784256 | bytes 6750208 | tf_op jit(solution)/shard_map/tdc,dcm->tm/dot_general | solution.py:120
  965.1 0.6 gather_fusion
  965.7 0.7 select_bitcast_fusion
  966.4 36.1 %reduce-scatter.2.cloned.1.call-done = bf16[64,512]{1,0:T(8,128)(2,1)} async-done(((bf16[64,2048]{1,0:T(8,128)(2,1)}), bf16[64,512]{1,0:T(8,128)(2,1)}) %reduce-scatter.2.cloned.1.call-update) | async-done | bytes 65552 | tf_op jit(solution)/shard_map/reduce_scatter | solution.py:121
  1002.5 1.6 add_convert_fusion.1
  (78 shorter events, 2.4 us)
Async XLA Ops:
  7.2 82.1 %copy-start = (bf16[512,2048]{1,0:T(8,128)(2,1)S(1)}, bf16[512,2048]{1,0:T(8,128)(2,1)}, u32[]{:S(2)}) copy-start(bf16[512,2048]{1,0:T(8,128)(2,1)} %param.21) | copy-start | bytes 6291460
  7.2 32.7 %copy-start.11 = (bf16[64,512]{1,0:T(8,128)(2,1)S(1)}, bf16[64,512]{1,0:T(8,128)(2,1)}, u32[]{:S(2)}) copy-start(bf16[64,512]{1,0:T(8,128)(2,1)} %param.15) | copy-start | bytes 196612
  7.2 34.1 %copy-start.12 = (s32[64,64]{1,0:T(8,128)S(1)}, s32[64,64]{1,0:T(8,128)}, u32[]{:S(2)}) copy-start(s32[64,64]{1,0:T(8,128)} %param.20) | copy-start | bytes 49156
  7.2 34.2 %copy-start.6 = (bf16[2,64,512]{2,1,0:T(8,128)(2,1)S(1)}, bf16[2,64,512]{2,1,0:T(8,128)(2,1)}, u32[]{:S(2)}) copy-start(bf16[2,64,512]{2,1,0:T(8,128)(2,1)} %param.16) | copy-start | bytes 393220
  7.2 36.3 %copy-start.16 = (s32[64,8]{0,1:T(8,128)S(1)}, s32[64,8]{0,1:T(8,128)}, u32[]{:S(2)}) copy-start(s32[64,8]{0,1:T(8,128)} %param.26) | copy-start | bytes 6148
  7.2 138.8 %all-reduce.2.cloned.1.call-start = ((), (), s32[]{:S(2)}) async-start(), calls=%async_computation.3 | async-start | bytes 524288 | tf_op jit(solution)/shard_map/psum | solution.py:91
  9.3 35.0 %collective-permute-start.4 = (bf16[2,2]{1,0:T(2,128)(2,1)}, bf16[2,2]{1,0:T(2,128)(2,1)}, u32[]{:S(2)}, u32[]{:S(2)}) collective-permute-start(bf16[2,2]{1,0:T(2,128)(2,1)} %pad_maximum_fusion), channel_id=1, source_target_pairs={{0,500},{4,504},{8,508},{12,0},{16,4},{20,8},{24,12},{28,16},{32,2... | collective-permute-start | bytes 32 | tf_op jit(solution)/shard_map/ppermute | solution.py:17
  17.0 33.8 %collective-permute-start.2 = (bf16[2,2]{1,0:T(2,128)(2,1)}, bf16[2,2]{1,0:T(2,128)(2,1)}, u32[]{:S(2)}, u32[]{:S(2)}) collective-permute-start(bf16[2,2]{1,0:T(2,128)(2,1)} %pad_maximum_fusion), channel_id=1, source_target_pairs={{0,504},{4,508},{8,0},{12,4},{16,8},{20,12},{24,16},{28,20},{32,24... | collective-permute-start | bytes 32 | tf_op jit(solution)/shard_map/ppermute | solution.py:17
  25.9 26.2 %collective-permute-start = (bf16[2,2]{1,0:T(2,128)(2,1)}, bf16[2,2]{1,0:T(2,128)(2,1)}, u32[]{:S(2)}, u32[]{:S(2)}) collective-permute-start(bf16[2,2]{1,0:T(2,128)(2,1)} %pad_maximum_fusion), channel_id=1, source_target_pairs={{0,508},{4,0},{8,4},{12,8},{16,12},{20,16},{24,20},{28,24},{32,28}... | collective-permute-start | bytes 32 | tf_op jit(solution)/shard_map/ppermute | solution.py:17
  29.9 42.0 %collective-permute-start.1 = (bf16[2,2,128,4,128]{4,2,1,3,0:T(8,128)(2,1)}, bf16[2,2,128,4,128]{4,2,1,3,0:T(8,128)(2,1)}, u32[]{:S(2)}, u32[]{:S(2)}) collective-permute-start(bf16[2,2,128,4,128]{4,2,1,3,0:T(8,128)(2,1)} %copy.162), channel_id=1, source_target_pairs={{0,508},{4,0},{8,4},{12,8},{16,12},{20,16},{24,20},{28,24},{32,28}... | collective-permute-start | bytes 1572872 | tf_op jit(solution)/shard_map/ppermute | solution.py:17
  32.9 33.7 %collective-permute-start.5 = (bf16[2,2,128,4,128]{4,2,1,3,0:T(8,128)(2,1)}, bf16[2,2,128,4,128]{4,2,1,3,0:T(8,128)(2,1)}, u32[]{:S(2)}, u32[]{:S(2)}) collective-permute-start(bf16[2,2,128,4,128]{4,2,1,3,0:T(8,128)(2,1)} %copy.162), channel_id=1, source_target_pairs={{0,500},{4,504},{8,508},{12,0},{16,4},{20,8},{24,12},{28,16},{32,2... | collective-permute-start | bytes 1572872 | tf_op jit(solution)/shard_map/ppermute | solution.py:17
  44.2 25.1 %collective-permute-start.3 = (bf16[2,2,128,4,128]{4,2,1,3,0:T(8,128)(2,1)}, bf16[2,2,128,4,128]{4,2,1,3,0:T(8,128)(2,1)S(1)}, u32[]{:S(2)}, u32[]{:S(2)}) collective-permute-start(bf16[2,2,128,4,128]{4,2,1,3,0:T(8,128)(2,1)} %copy.162), channel_id=1, source_target_pairs={{0,504},{4,508},{8,0},{12,4},{16,8},{20,12},{24,16},{28,20},{32,24... | collective-permute-start | bytes 1572872 | tf_op jit(solution)/shard_map/ppermute | solution.py:17
  54.1 13.8 %copy-start.18 = (pred[2,128]{1,0:T(4,128)(4,1)}, pred[2,128]{1,0:T(4,128)(4,1)S(1)}, u32[]{:S(2)}) copy-start(pred[2,128]{1,0:T(4,128)(4,1)S(1)} %get-tuple-element.26) | copy-start | bytes 772
  54.1 20.3 %copy-start.17 = (pred[2,128]{1,0:T(4,128)(4,1)}, pred[2,128]{1,0:T(4,128)(4,1)S(1)}, u32[]{:S(2)}) copy-start(pred[2,128]{1,0:T(4,128)(4,1)S(1)} %get-tuple-element.24) | copy-start | bytes 772
  67.9 4.1 copy-start.13
  69.3 2.6 copy-start.10
  70.5 1.5 copy-start.14
  85.1 60.9 %copy-start.2 = (bf16[64,2048]{1,0:T(8,128)(2,1)S(1)}, bf16[64,2048]{1,0:T(8,128)(2,1)}, u32[]{:S(2)}) copy-start(bf16[64,2048]{1,0:T(8,128)(2,1)} %param.14) | copy-start | bytes 786436
  87.5 60.4 %copy-start.15 = (f32[2048]{0:T(1024)S(1)}, f32[2048]{0:T(1024)}, u32[]{:S(2)}) copy-start(f32[2048]{0:T(1024)} %param.22) | copy-start | bytes 24580
  89.3 60.6 %copy-start.9 = (bf16[64,512]{1,0:T(8,128)(2,1)}, bf16[64,512]{1,0:T(8,128)(2,1)S(1)}, u32[]{:S(2)}) copy-start(bf16[64,512]{1,0:T(8,128)(2,1)S(1)} %copy_bitcast_fusion) | copy-start | bytes 196612
  537.7 10.8 %copy-start.8 = (bf16[2,2048,128]{2,1,0:T(8,128)(2,1)S(1)}, bf16[2,2048,128]{2,1,0:T(8,128)(2,1)}, u32[]{:S(2)}) copy-start(bf16[2,2048,128]{2,1,0:T(8,128)(2,1)} %param.24) | copy-start | bytes 3145732
  548.5 4.7 copy-start.4
  575.6 13.1 %copy-start.20 = (s32[8]{0:T(128)S(1)}, s32[8]{0:T(128)}, u32[]{:S(2)}) copy-start(s32[8]{0:T(128)} %param.27) | copy-start | bytes 100
  575.6 13.1 %copy-start.3 = (bf16[64,2048]{1,0:T(8,128)(2,1)S(1)}, bf16[64,2048]{1,0:T(8,128)(2,1)}, u32[]{:S(2)}) copy-start(bf16[64,2048]{1,0:T(8,128)(2,1)} %all-reduce.2.cloned.1.call-done) | copy-start | bytes 786436
  575.6 13.1 %copy-start.19 = (bf16[2048,64]{0,1:T(8,128)(2,1)S(1)}, bf16[2048,64]{0,1:T(8,128)(2,1)}, u32[]{:S(2)}) copy-start(bf16[2048,64]{0,1:T(8,128)(2,1)} %param.23) | copy-start | bytes 786436
  575.6 13.4 %copy-start.5 = (s32[64,8]{1,0:T(8,128)S(1)}, s32[64,8]{1,0:T(8,128)}, u32[]{:S(2)}) copy-start(s32[64,8]{1,0:T(8,128)} %copy.180) | copy-start | bytes 6148
  575.6 378.0 %all-to-all-start.1 = ((bf16[128,12,2048]{2,1,0:T(8,128)(2,1)}), bf16[128,12,2048]{2,1,0:T(8,128)(2,1)}, u32[]{:S(2)}, u32[]{:S(2)}) async-start(bf16[128,12,2048]{2,1,0:T(8,128)(2,1)} %reshape.368), calls=%async_computation.1 | async-start | bytes 16777216 | tf_op jit(solution)/shard_map/all_to_all | solution.py:37
  588.4 414.2 %reduce-scatter.2.cloned.1.call-start = ((), (), s32[]{:S(2)}) async-start(), calls=%async_computation.4 | async-start | bytes 327680 | tf_op jit(solution)/shard_map/reduce_scatter | solution.py:121
  953.8 11.2 %copy-start.7 = (bf16[2,64,512]{2,1,0:T(8,128)(2,1)S(1)}, bf16[2,64,512]{2,1,0:T(8,128)(2,1)}, u32[]{:S(2)}) copy-start(bf16[2,64,512]{2,1,0:T(8,128)(2,1)} %param.16) | copy-start | bytes 393220
  953.9 50.3 %copy-start.1 = (bf16[512,2048]{1,0:T(8,128)(2,1)S(1)}, bf16[512,2048]{1,0:T(8,128)(2,1)}, u32[]{:S(2)}) copy-start(bf16[512,2048]{1,0:T(8,128)(2,1)} %param.21) | copy-start | bytes 6291460
Sparse Core Ops, SparseCore 0:
  90.6 55.3 all-reduce.1
  965.2 37.3 reduce-scatter.1
where the time goes:
time: 1010 us
  waiting for transfers between devices  465 us (46%)
  blocking collectives  382 us (38%)
  starting transfers between devices  44 us (4%)
  matrix products  43.1 us (4%)
  local copies, waits for them, and re-layouts  41.4 us (4%)
  other arithmetic  21.6 us (2%)
  between operations  14.6 us (1%)
    all_to_all x1, blocking collectives, body(): lax.all_to_all(outgoing, 'req', split_axis=0, concat_axis=0, tiled=True)  382 us
    all_to_all x1, waiting for transfers between devices, finish_expert(): lax.all_to_all(result, 'req', split_axis=0, concat_axis=0, tiled=True)  364 us
    psum x1, waiting for transfers between devices, body(): lax.psum(partial_proj.astype(jnp.bfloat16), 'tp').astype(jnp.float32)  54.2 us
    reduce_scatter x1, waiting for transfers between devices, body(): lax.psum_scatter(moe_part.astype(jnp.bfloat16), 'tp', scatter_dimension=1...  36.1 us
    ppermute x6, starting transfers between devices, passed_along(): lax.ppermute(value, axis, [(i, (i + by) % devices) for i in range(devices)])  30.9 us
  transfers between devices with their start and end apart: 9, of which 4 were waited for; matrix products, arithmetic and copies ran while one was open for 2% of the time, Pallas kernels for 0%

commit v1 on v0

v1 whole, which is shorter than its diff:
```python
import functools

import jax
import jax.numpy as jnp
from jax import lax
from jax.experimental import pallas as pl
from jax.experimental.pallas import tpu as pltpu
from jax.sharding import PartitionSpec as P

HD = 128
HEADS = 4
PIECES = 2
PIECE = 128
SPAN = 4
T = 64
C = 512
D = 2048
CAP = 12
Z = 16
N_REQ = 128
NEG = -1e30
NONE = -100.0
F32 = jnp.float32
BF16 = jnp.bfloat16
MESH = pl.DeviceIdType.MESH

ORDER = [0, 1, -1, 2, -2, 3, -3, 4, -4, 5, -5, 6, -6, 7, -7, 8]
POS = {rel: at for at, rel in enumerate(ORDER)}
FLIPS = [(a, b, h) for h in (0, 1) for a in (0, 1) for b in (0, 1)]


def iota(shape, dim):
    return lax.broadcasted_iota(jnp.int32, shape, dim)


def nt(a, b):
    return lax.dot_general(a, b, (((1,), (1,)), ((), ())), preferred_element_type=F32)


def tn(a, b):
    return lax.dot_general(a, b, (((0,), (0,)), ((), ())), preferred_element_type=F32)


def nn(a, b):
    return jnp.dot(a, b, preferred_element_type=F32)


def softmax_part(scores, mask, values):
    top = jnp.max(jnp.where(mask, scores, NEG), axis=1, keepdims=True)
    weights = jnp.where(mask, jnp.exp(scores - top), 0.0)
    total = jnp.sum(weights, axis=1, keepdims=True)
    return top, total, nn(weights.astype(BF16), values)


def kernel(
    q_ref, dkv_ref, ckv_ref, off_ref, len_ref, anc_ref, hid_ref, op_ref, gain_ref, rw_ref,
    gu_ref, dn_ref, ids_ref, accid_ref,
    out_ref, att_ref, acc_ref,
    w_all, d_all, q_in, part_out, stat_out, part_in, stat_in, proj_out, proj_in,
    code_out, code_in, gate_out, gate_in, rows, full, hot, packed, x_in, normed, act, o_out, t_in,
    moe, rs_out, rs_in,
    wl_sem, ws_sem, wr_sem, qs_sem, qr_sem, ps_sem, pr_sem, as_sem, ar_sem, fs_sem, fr_sem,
    cs_sem, cr_sem, gs_sem, gr_sem, zs_sem, zr_sem, ds_sem, dr_sem, ts_sem, tr_sem, ss_sem, sr_sem,
):
    req, tp = lax.axis_index("req"), lax.axis_index("tp")
    z, yl, x = req // 8, (req // 4) % 2, req % 4
    xh, xl = x // 2, x % 2
    yh, c = tp // 2, tp % 2
    scale = HD ** (-0.5)
    sends = []

    def along(k):
        return (lax.rem(req + (k + N_REQ), N_REQ), tp)

    def plane(d):
        return (lax.rem(z + (d + Z), Z) * 8 + yl * 4 + x, tp)

    def flipped(a, b, h, core):
        y2 = 1 - yl if a else yl
        x2 = 3 - x if b else x
        h2 = 1 - yh if h else yh
        return (z * 8 + y2 * 4 + x2, h2 * 2 + core)

    x_partner = (req + 1 - 2 * xl, tp)
    core_partner = (req, yh * 2 + 1 - c)

    def copy(src, dst, send, recv, to):
        return pltpu.make_async_remote_copy(
            src_ref=src, dst_ref=dst, send_sem=send, recv_sem=recv, device_id=to, device_id_type=MESH
        )

    def send(src, dst, send_sem, recv_sem, to):
        one = copy(src, dst, send_sem, recv_sem, to)
        one.start()
        sends.append(one)

    def arrived(dst, send_sem, recv_sem):
        copy(dst, dst, send_sem, recv_sem, core_partner).wait_recv()

    ids = ids_ref[...].astype(F32).astype(BF16)
    eye = (iota((16, 8), 0) == iota((16, 8), 1)).astype(F32).astype(BF16)
    ids_t = nt(eye, ids)
    n_row = iota((128, T), 0)
    j_row = n_row & 7
    e_row = (n_row >> 3) * 4 + ((yl + (j_row >> 1)) & 1) * 2 + ((xh + j_row) & 1)
    e_row = jnp.where(j_row < 4, e_row, -1)
    e_rowf = e_row.astype(F32)
    routed_t = jnp.zeros((128, T), F32)
    for j in range(8):
        routed_t += (ids_t[j : j + 1, :] == e_rowf).astype(F32)
    routed_t = routed_t.astype(BF16)
    place = []
    for par in (0, 1):
        lane = iota((T, 128), 1) - T * par
        t_row = iota((T, 128), 0)
        later = ((lane > t_row) & (lane < T)).astype(F32).astype(BF16)
        same = (lane == t_row).astype(F32).astype(BF16)
        place.append(same)
        rank = nn(routed_t, later)
        there = nn(routed_t, same)
        code_out[par] = jnp.where(there > 0.5, rank, NONE).reshape(Z, 8, 128)

    barrier = pltpu.get_barrier_semaphore()
    peers = [along(k) for k in (1, 2, 3, -1, -2, -3)]
    peers += [plane(d) for d in range(-8, 8) if d]
    peers += [flipped(a, b, h, 1 - c) for a, b, h in FLIPS]
    peers += [flipped(a, b, h, c) for a, b, h in FLIPS if a or b or h]
    peers += [x_partner]
    for peer in peers:
        pl.semaphore_signal(barrier, inc=1, device_id=peer, device_id_type=MESH)
    pl.semaphore_wait(barrier, len(peers))

    for k in (1, 2, 3):
        send(q_ref, q_in.at[k], qs_sem.at[k], qr_sem.at[k], along(k))
    for d in range(-8, 8):
        if d:
            at = POS[-d]
            to_z = lax.rem(z + (d + Z), Z)
            send(code_out.at[at % 2, to_z], code_in.at[at], cs_sem.at[at], cr_sem.at[at], plane(d))
    code_in[0] = code_out[0, z]
    q_in[0] = q_ref[...]

    local = [
        pltpu.make_async_copy(gu_ref.at[0], w_all.at[0, :, 0:128], wl_sem.at[0]),
        pltpu.make_async_copy(gu_ref.at[1], w_all.at[0, :, 128:256], wl_sem.at[1]),
        pltpu.make_async_copy(dn_ref, d_all.at[0:128], wl_sem.at[2]),
    ]
    for one in local:
        one.start()
    for slot, to in ((1, core_partner), (2, x_partner)):
        for i in (0, 1):
            send(gu_ref.at[i], w_all.at[slot, :, i * 128 : i * 128 + 128],
                 ws_sem.at[slot, i], wr_sem.at[slot, i], to)
        send(dn_ref, d_all.at[slot * 128 : slot * 128 + 128], ws_sem.at[slot, 2], wr_sem.at[slot, 2], to)

    tree = anc_ref[...] > 0
    draft = []
    for h in range(HEADS):
        cols = slice(h * HD, h * HD + HD)
        scores = nt(q_ref[:, cols], dkv_ref[0, :, cols]) * scale
        draft.append(softmax_part(scores, tree, dkv_ref[1, :, cols]))

    pick = jnp.zeros((16, 128), jnp.int32)
    a_row = iota((16, 128), 0)
    for i in range(8):
        pick = jnp.where((a_row & 7) == i, accid_ref[i], pick)
    pick = pick + T * (a_row >> 3)
    chosen = (iota((16, 128), 1) == pick).astype(F32).astype(BF16)
    acc_ref[...] = nn(chosen, dkv_ref[...].reshape(128, C)).astype(BF16)

    for k in (1, 2, 3):
        arrived(q_in.at[k], qs_sem.at[k], qr_sem.at[k])
    parts = []
    for p in range(PIECES):
        query = q_in[off_ref[p]]
        valid = iota((T, PIECE), 1) < len_ref[p]
        mine = []
        for h in range(HEADS):
            cols = slice(h * HD, h * HD + HD)
            slots = slice(p * PIECE, p * PIECE + PIECE)
            scores = nt(query[:, cols], ckv_ref[0, slots, cols]) * scale
            mine.append(softmax_part(scores, valid, ckv_ref[1, slots, cols]))
        parts.append(mine)
    lanes = iota((T, 128), 1)
    own = []
    for k in (1, 2, 3, 0):
        stats = jnp.zeros((T, 128), F32)
        for h in range(HEADS):
            tops = [jnp.where(off_ref[p] == k, parts[p][h][0], NEG) for p in range(PIECES)]
            top = jnp.maximum(tops[0], tops[1])
            total, acc = 0.0, 0.0
            for p in range(PIECES):
                factor = jnp.where(off_ref[p] == k, jnp.exp(tops[p] - top), 0.0)
                total = total + factor * parts[p][h][1]
                acc = acc + factor * parts[p][h][2]
            if k == 0:
                own.append((top, total, acc))
                continue
            part_out[k, :, h * HD : h * HD + HD] = acc.astype(BF16)
            stats = jnp.where(lanes == h, top, stats)
            stats = jnp.where(lanes == 4 + h, total, stats)
        if k:
            stat_out[k] = stats
            send(part_out.at[k], part_in.at[k], ps_sem.at[0, k], pr_sem.at[0, k], along(-k))
            send(stat_out.at[k], stat_in.at[k], ps_sem.at[1, k], pr_sem.at[1, k], along(-k))

    for k in (1, 2, 3):
        arrived(part_in.at[k], ps_sem.at[0, k], pr_sem.at[0, k])
        arrived(stat_in.at[k], ps_sem.at[1, k], pr_sem.at[1, k])
    for h in range(HEADS):
        cols = slice(h * HD, h * HD + HD)
        every = [draft[h], own[h]]
        for k in (1, 2, 3):
            stats = stat_in[k]
            every.append((stats[:, h : h + 1], stats[:, 4 + h : 5 + h], part_in[k, :, cols].astype(F32)))
        best = every[0][0]
        for top, _, _ in every[1:]:
            best = jnp.maximum(best, top)
        total, acc = 0.0, 0.0
        for top, one_total, one_acc in every:
            factor = jnp.exp(top - best)
            total = total + factor * one_total
            acc = acc + factor * one_acc
        att_ref[:, cols] = (acc / total).astype(BF16)

    attended = att_ref[...]
    for q in range(4):
        proj_out[q] = nn(attended, op_ref[:, q * C : q * C + C])
    others = [(1, 1), (1, 0), (0, 1)]
    for i, (h, k) in enumerate(others):
        core = 1 - c if k else c
        tp2 = (1 - yh if h else yh) * 2 + core
        part_out[4 + i] = proj_out[tp2].astype(BF16)
        send(part_out.at[4 + i], proj_in.at[i], as_sem.at[i], ar_sem.at[i], (req, tp2))
    cols = pl.ds(pl.multiple_of(tp * C, C), C)
    total = hid_ref[:, cols].astype(F32) + proj_out[tp]
    for i in range(3):
        arrived(proj_in.at[i], as_sem.at[i], ar_sem.at[i])
        total = total + proj_in[i].astype(F32)
    residual = total.astype(BF16)
    rows[0] = residual

    def pass_on(rel):
        step = 1 if rel <= 0 else -1
        new = rel - step
        send(rows.at[POS[rel]], rows.at[POS[new]], zs_sem.at[POS[new]], zr_sem.at[POS[new]], plane(step))

    def rows_arrived(rel):
        arrived(rows.at[POS[rel]], zs_sem.at[POS[rel]], zr_sem.at[POS[rel]])

    pass_on(0)
    send(rows.at[0], rows.at[POS[1]], zs_sem.at[POS[1]], zr_sem.at[POS[1]], plane(-1))
    full[tp] = residual
    for i, (h, k) in enumerate(others):
        core = 1 - c if k else c
        tp2 = (1 - yh if h else yh) * 2 + core
        send(rows.at[0], full.at[tp], fs_sem.at[i], fr_sem.at[i], (req, tp2))

    for d in range(-8, 8):
        if d:
            at = POS[-d]
            arrived(code_in.at[at], cs_sem.at[at], cr_sem.at[at])

    def hot_group(n):
        for j in range(4):
            for pair in (0, 1):
                at = 4 * n + 2 * pair
                line = jnp.maximum(
                    code_in[at, j : j + 1, :] + CAP * 2.0 * pair,
                    code_in[at + 1, j : j + 1, :] + CAP * (2.0 * pair + 1.0),
                )
                match = iota((48, 128), 0).astype(F32) == line
                hot[n, j * 48 : j * 48 + 48, pair * 128 : pair * 128 + 128] = match.astype(F32).astype(BF16)

    for n in range(4):
        hot_group(n)

    def gates():
        for i, (h, k) in enumerate(others):
            core = 1 - c if k else c
            tp2 = (1 - yh if h else yh) * 2 + core
            arrived(full.at[tp2], fs_sem.at[i], fr_sem.at[i])
        square = jnp.zeros((T, 1), F32)
        for q in range(4):
            part = full[q].astype(F32)
            square = square + jnp.sum(part * part, axis=1, keepdims=True)
        inverse = lax.rsqrt(square * (1.0 / D) + 1e-06)
        logits = jnp.zeros((T, 64), F32)
        for q in range(4):
            some = (full[q].astype(F32) * inverse * gain_ref[:, q * C : q * C + C]).astype(BF16)
            logits = logits + nn(some, rw_ref[q * C : q * C + C, :])
        named = jnp.zeros((T, 64), F32)
        ids_i = ids_ref[...]
        for j in range(8):
            named = named + (ids_i[:, j : j + 1] == iota((T, 64), 1)).astype(F32)
        top = jnp.max(jnp.where(named > 0.5, logits, NEG), axis=1, keepdims=True)
        weight = jnp.where(named > 0.5, jnp.exp(logits - top), 0.0)
        gate = (weight / jnp.sum(weight, axis=1, keepdims=True)).astype(BF16)
        n2 = iota((128, 64), 0)
        j2 = n2 & 7
        e2 = (n2 >> 3) * 4 + ((yl + (j2 >> 1)) & 1) * 2 + ((xh + j2) & 1)
        select = ((j2 < 4) & (e2 == iota((128, 64), 1))).astype(F32).astype(BF16)
        gate_t = nt(select, gate).astype(BF16)
        for par in (0, 1):
            gate_out[par] = nn(gate_t, place[par]).reshape(Z, 8, 128)
        for d in range(-8, 8):
            if d:
                at = POS[-d]
                to_z = lax.rem(z + (d + Z), Z)
                send(gate_out.at[at % 2, to_z], gate_in.at[at], gs_sem.at[at], gr_sem.at[at], plane(d))
        gate_in[0] = gate_out[0, z]

    def x_cols(core, h=None):
        tp2 = yh * 2 + core if h is None else (1 - yh if h else yh) * 2 + core
        return pl.ds(pl.multiple_of(tp2 * C, C), C)

    special = []

    def dispatch(n):
        packed[n] = nn(hot[n], rows[4 * n : 4 * n + 4].reshape(256, C)).astype(BF16)
        m, core = n // 2, n % 2
        for i, (a, b, h) in enumerate(FLIPS):
            j = a * 2 + b
            src = packed.at[n, j * 48 : j * 48 + 48]
            dst = x_in.at[m, j * 48 : j * 48 + 48, x_cols(c)]
            if i:
                send(src, dst, ds_sem.at[n, i], dr_sem.at[m, i, c], flipped(a, b, h, core))
                continue

            @pl.when(c == core)
            def _():
                dst[...] = src[...]

            one = copy(src, dst, ds_sem.at[n, i], dr_sem.at[m, i, c], (req, yh * 2 + 1 - c))

            @pl.when(c != core)
            def _():
                one.start()

            special.append((core, one))

    for s in range(1, 9):
        if s < 8:
            rows_arrived(-s)
            if s < 7:
                pass_on(-s)
        rows_arrived(s)
        if s < 8:
            pass_on(s)
        if s % 2 == 0:
            dispatch(s // 2 - 1)
        if s == 3:
            gates()
        if s == 7:
            for i in (0, 1):
                arrived(w_all.at[2, :, i * 128 : i * 128 + 128], ws_sem.at[2, i], wr_sem.at[2, i])
            arrived(d_all.at[256:384], ws_sem.at[2, 2], wr_sem.at[2, 2])
            send(w_all.at[2], w_all.at[3], ws_sem.at[3, 0], wr_sem.at[3, 0], core_partner)
            send(d_all.at[256:384], d_all.at[384:512], ws_sem.at[3, 1], wr_sem.at[3, 1], core_partner)

    for one in local:
        one.wait()
    for i in (0, 1):
        arrived(w_all.at[1, :, i * 128 : i * 128 + 128], ws_sem.at[1, i], wr_sem.at[1, i])
    arrived(d_all.at[128:256], ws_sem.at[1, 2], wr_sem.at[1, 2])
    arrived(w_all.at[3], ws_sem.at[3, 0], wr_sem.at[3, 0])
    arrived(d_all.at[384:512], ws_sem.at[3, 1], wr_sem.at[3, 1])

    for m in (0, 1):
        for i, (a, b, h) in enumerate(FLIPS):
            j = a * 2 + b
            for k in (0, 1):
                if i or k:
                    core = 1 - c if k else c
                    arrived(x_in.at[m, j * 48 : j * 48 + 48, x_cols(core, h)],
                            ds_sem.at[0, i], dr_sem.at[m, i, core])

        @pl.loop(0, 4)
        def _(j):
            some = pl.ds(pl.multiple_of(j * 48, 16), 48)
            block = x_in[m, some, :].astype(F32)
            mean = jnp.sum(block * block, axis=1, keepdims=True) * (1.0 / D)
            normed[some, :] = (block * lax.rsqrt(mean + 1e-06) * gain_ref[...]).astype(BF16)

        @pl.loop(0, 4)
        def _(j):
            both = nn(normed[...], w_all[j])
            gate, upper = both[:, :128], both[:, 128:]
            hidden = gate / (1.0 + jnp.exp(-gate)) * upper
            act[:, pl.ds(pl.multiple_of(j * 128, 128), 128)] = hidden.astype(BF16)

        @pl.loop(0, 4)
        def _(q):
            some = pl.ds(pl.multiple_of(q * C, C), C)
            o_out[m, :, some] = nn(act[...], d_all[:, some]).astype(BF16)

        for i, (a, b, h) in enumerate(FLIPS):
            j = a * 2 + b
            for k in (0, 1):
                core = 1 - c if k else c
                src = o_out.at[m, j * 48 : j * 48 + 48, x_cols(core, h)]
                dst = t_in.at[2 * m + c, h, j * 48 : j * 48 + 48]
                if i or k:
                    send(src, dst, ts_sem.at[m, i, k], tr_sem.at[2 * m + c, i], flipped(a, b, h, core))
                else:
                    dst[...] = src[...]

    for d in range(-8, 8):
        if d:
            at = POS[-d]
            arrived(gate_in.at[at], gs_sem.at[at], gr_sem.at[at])

    def combine(n):
        for i, (a, b, h) in enumerate(FLIPS):
            j = a * 2 + b

            def wait(i=i, h=h, j=j):
                arrived(t_in.at[n, h, j * 48 : j * 48 + 48], ts_sem.at[0, i, 0], tr_sem.at[n, i])

            if i:
                wait()
            else:
                pl.when(c != n % 2)(wait)
        blocks = []
        for j in range(4):
            halves = []
            for pair in (0, 1):
                at = 4 * n + 2 * pair
                gate = gate_in[at, j : j + 1, :] + gate_in[at + 1, j : j + 1, :]
                some = hot[n, j * 48 : j * 48 + 48, pair * 128 : pair * 128 + 128].astype(F32)
                halves.append(some * gate)
            blocks.append(jnp.concatenate(halves, axis=1))
        weight = jnp.concatenate(blocks, axis=0).astype(BF16)
        result = tn(weight, t_in[n, 0]) + tn(weight, t_in[n, 1])
        moe[4 * n : 4 * n + 4] = result.reshape(4, T, C)

    def sum_on(rel):
        step = 1 if rel > 0 else -1
        here = moe[POS[rel]]
        before = rel + step
        if before in POS and before != -8:
            arrived(rs_in.at[POS[rel]], ss_sem.at[POS[rel]], sr_sem.at[POS[rel]])
            here = here + rs_in[POS[rel]].astype(F32)
        rs_out[POS[rel]] = here.astype(BF16)
        slot = POS[rel - step] if rel - step else (0 if step > 0 else 16)
        send(rs_out.at[POS[rel]], rs_in.at[slot], ss_sem.at[POS[rel]], sr_sem.at[slot], plane(step))

    for n in (3, 2, 1, 0):
        combine(n)
        far = sorted(ORDER[4 * n : 4 * n + 4], key=lambda r: -abs(r))
        for rel in far:
            if rel:
                sum_on(rel)
    total = rows[0].astype(F32) + moe[0]
    for slot in (0, 16):
        arrived(rs_in.at[slot], ss_sem.at[1], sr_sem.at[slot])
        total = total + rs_in[slot].astype(F32)
    out_ref[...] = total.astype(BF16)

    for one in sends:
        one.wait_send()
    for core, one in special:

        @pl.when(c != core)
        def _(one=one):
            one.wait_send()


def body(
    hidden, draft_query, draft_kv, cache_kv, piece_offset, piece_length, ancestors, out_proj,
    ffn_gain, router_w, expert_gate_up, expert_down, expert_ids, accepted_ids,
):
    vmem = pl.BlockSpec(memory_space=pltpu.VMEM)
    smem = pl.BlockSpec(memory_space=pltpu.SMEM)
    hbm = pl.BlockSpec(memory_space=pl.ANY)
    dma = pltpu.SemaphoreType.DMA
    layer_out, attended, accepted = pl.pallas_call(
        kernel,
        out_shape=(
            jax.ShapeDtypeStruct((T, C), BF16),
            jax.ShapeDtypeStruct((T, C), BF16),
            jax.ShapeDtypeStruct((16, C), BF16),
        ),
        in_specs=[vmem, vmem, vmem, smem, smem, vmem, vmem, vmem, vmem, vmem, hbm, hbm, vmem, smem],
        out_specs=(vmem, vmem, vmem),
        scratch_shapes=[
            pltpu.VMEM((4, D, 256), BF16),
            pltpu.VMEM((512, D), BF16),
            pltpu.VMEM((4, T, C), BF16),
            pltpu.VMEM((7, T, C), BF16),
            pltpu.VMEM((4, T, 128), F32),
            pltpu.VMEM((4, T, C), BF16),
            pltpu.VMEM((4, T, 128), F32),
            pltpu.VMEM((4, T, C), F32),
            pltpu.VMEM((3, T, C), BF16),
            pltpu.VMEM((2, Z, 8, 128), F32),
            pltpu.VMEM((Z, 8, 128), F32),
            pltpu.VMEM((2, Z, 8, 128), F32),
            pltpu.VMEM((Z, 8, 128), F32),
            pltpu.VMEM((Z, T, C), BF16),
            pltpu.VMEM((4, T, C), BF16),
            pltpu.VMEM((4, 192, 256), BF16),
            pltpu.VMEM((4, 192, C), BF16),
            pltpu.VMEM((2, 192, D), BF16),
            pltpu.VMEM((192, D), BF16),
            pltpu.VMEM((192, 512), BF16),
            pltpu.VMEM((2, 192, D), BF16),
            pltpu.VMEM((4, 2, 192, C), BF16),
            pltpu.VMEM((Z, T, C), F32),
            pltpu.VMEM((Z, T, C), BF16),
            pltpu.VMEM((Z + 1, T, C), BF16),
            dma((3,)), dma((4, 3)), dma((4, 3)), dma((4,)), dma((4,)),
            dma((2, 4)), dma((2, 4)), dma((3,)), dma((3,)), dma((3,)), dma((3,)),
            dma((Z,)), dma((Z,)), dma((Z,)), dma((Z,)), dma((Z,)), dma((Z,)),
            dma((4, 8)), dma((2, 8, 2)), dma((2, 8, 2)), dma((4, 8)), dma((Z,)), dma((Z + 1,)),
        ],
        compiler_params=pltpu.CompilerParams(
            collective_id=0, has_side_effects=True, vmem_limit_bytes=56 * 2**20
        ),
        cost_estimate=pl.CostEstimate(flops=3 * 10**9, bytes_accessed=6 * 10**6, transcendentals=10**6),
        name="layer",
    )(
        draft_query, draft_kv, cache_kv, piece_offset, piece_length, ancestors, hidden, out_proj,
        ffn_gain.reshape(1, D), router_w, expert_gate_up, expert_down, expert_ids, accepted_ids,
    )
    return layer_out, attended, accepted.reshape(2, 8, C)


def solution(mesh):
    in_specs = (
        P("req", None),
        P("req", "tp"),
        P(None, "req", "tp"),
        P(None, "req", "tp"),
        P("req"),
        P("req"),
        P("req", None),
        P("tp", None),
        P(),
        P(),
        P(None, None, ("req", "tp")),
        P(("req", "tp"), None),
        P("req", None),
        P("req"),
    )
    out_specs = (P("req", "tp"), P("req", "tp"), P(None, "req", "tp"))
    return jax.shard_map(body, mesh=mesh, in_specs=in_specs, out_specs=out_specs, check_vma=False)
```

time: 1010 us -> 165 us (0.16)
  waiting for transfers between devices: 465 us -> 0 us
  blocking collectives: 382 us -> 0 us
  Pallas kernels: 0 us -> 157 us
  starting transfers between devices: 44 us -> 0 us
  matrix products: 43.1 us -> 0 us
  local copies, waits for them, and re-layouts: 41.4 us -> 7.6 us
  other arithmetic: 21.6 us -> 0 us
  between operations: 14.6 us -> 0.64 us
    all_to_all x1 -> x0, blocking collectives: 382 us -> none  [body(): lax.all_to_all(outgoing, 'req', split_axis=0, concat_axis=0, tiled=True)]
    all_to_all x1 -> x0, waiting for transfers between devices: 364 us -> none  [finish_expert(): lax.all_to_all(result, 'req', split_axis=0, concat_axis=0, tiled=True)]
    pallas_call x0 -> x1, Pallas kernels: none -> 157 us  [body(): pl.pallas_call(kernel, out_shape=(jax.ShapeDtypeStruct((T, C), BF16), jax...]
    psum x1 -> x0, waiting for transfers between devices: 54.2 us -> none  [body(): lax.psum(partial_proj.astype(jnp.bfloat16), 'tp').astype(jnp.float32)]
    dot_general x16 -> x0, matrix products: 43.1 us -> none  [the longest x1 11.9 us: finish_expert(): jnp.dot(act, expert_down, preferred_element_type=jnp.float32)]
    reduce_scatter x1 -> x0, waiting for transfers between devices: 36.1 us -> none  [body(): lax.psum_scatter(moe_part.astype(jnp.bfloat16), 'tp', scatter_dimension=1...]
    ppermute x6 -> x0, starting transfers between devices: 30.9 us -> none  [passed_along(): lax.ppermute(value, axis, [(i, (i + by) % devices) for i in range(devices)])]
    reshape x5 -> x0, local copies, waits for them, and re-layouts: 24.1 us -> none  [the longest x1 10.8 us: body(): flat = received.reshape(-1, received.shape[2])]
  transfers between devices with their start and end apart: 9 -> 0, of which waited for: 4 -> 0; matrix products, arithmetic and copies ran while one was open for 2% -> 0% of each run, Pallas kernels for 0% -> 0%
where the time goes in v1:
time: 165 us
  Pallas kernels  157 us (95%)
  local copies, waits for them, and re-layouts  7.6 us (5%)
    pallas_call x1, Pallas kernels, body(): pl.pallas_call(kernel, out_shape=(jax.ShapeDtypeStruct((T, C), BF16), jax...  157 us
    unnamed x5, local copies, waits for them, and re-layouts  7.6 us

profile of v1, /device:TPU:6, one launch (start us, length us, event | category | flops | bytes accessed | tf_op | source)
XLA Modules:
  0.0 165.1 jit_solution(7120622844753140967)
XLA Ops:
  0.6 1.4 copy.18.ids_ref
  2.0 1.9 %copy.17.rw_ref = bf16[2048,64]{1,0:T(8,128)(2,1)} copy(bf16[2048,64]{0,1:T(8,128)(2,1)} %param.23) | data formatting | bytes 524288 | tf_op args[9]
  4.0 156.8 %layer.1 = (bf16[64,512]{1,0:T(8,128)(2,1)}, bf16[64,512]{1,0:T(8,128)(2,1)}, bf16[16,512]{1,0:T(8,128)(2,1)}) custom-call(bf16[64,512]{1,0:T(8,128)(2,1)} %q_ref.1, bf16[2,64,512]{2,1,0:T(8,128)(2,1)} %dkv_ref.1, bf16[2,256,512]{2,1,0:T(8,128)(2,1)} %ckv_ref.1, s32[2]{0:T(128)} %off_ref.1, s32[2]{0:T(128)} %len_ref.1, s32[64,64]{1,0:T(8,128)} %anc_ref.1, ...), custom_call_target="tpu_custom_call" | custom-call | flops 3000000000 | bytes 6000000 | tf_op jit(solution)/shard_map/layer/pallas_call | solution.py:477
  160.8 1.5 copy.22
  162.3 1.5 copy.23
  163.8 1.3 copy.24
